TPU v7x, 32 devices: a whole 2x2x4 slice. The times are simulated.
32 devices in a mesh: grp: 2 (over x), gx: 16 (over z, y, core).
Axes of the slice: x: 2, y: 2, z: 4, core: 2. Of those that a mesh axis runs over, the one named last changes fastest.
Arguments:
- permeability: float32 [256, 64, 128], P('gx', 'grp'), parts along dimension 1, may hold values from 0.1 to 10
- sources: float32 [8, 256, 64, 128], P(None, 'gx', 'grp'), parts along dimension 2, may hold values from -1 to 2
Outputs:
- block_stiffness: float32 [8, 8, 16, 4, 8], P(None, None, 'gx', 'grp'), parts along dimension 3
- face_stiffness: float32 [3, 8, 8, 16, 4, 8], P(None, None, None, 'gx', 'grp'), parts along dimension 4
There are 2 independent parts, one for each index of `grp`. A program takes and returns all parts, laid end to end along the dimension named above; each array names one. Nothing has to cross between parts.
All inputs are finite; a program needn't handle non-finite values.
Results may differ from a plain program's by a relative error of at most 0.0049.
Values sent between devices are 32-bit elements; how exact they have to be, the bound alone decides.
A program may use at most 256 MiB of HBM per device.

v0:
```python
import jax
import jax.numpy as jnp
from jax import lax
from jax.sharding import PartitionSpec as P

B = 16
SWEEPS = 4


WEIGHT_Z = 0.1


def extended_2(block, sides, width):
    for axis, dim in sides:
        count = lax.axis_size(axis)
        forward = [(i, i + 1) for i in range(count - 1)]
        backward = [(target, source) for source, target in forward]
        low = lax.ppermute(
            lax.slice_in_dim(block, block.shape[dim] - width, None, axis=dim), axis, forward
        )
        high = lax.ppermute(lax.slice_in_dim(block, 0, width, axis=dim), axis, backward)
        block = jnp.concatenate([low, block, high], axis=dim)
    return block


def from_behind(x, axis, by):
    length = lax.axis_size(axis)
    pairs = [(i, i + by) for i in range(length) if 0 <= i + by < length]
    return lax.ppermute(x, axis, pairs)


def conduct(perm_field):
    padded = jnp.pad(perm_field, 1)
    face_x = 0.5 * (padded[1:, 1:-1, 1:-1] + padded[:-1, 1:-1, 1:-1])
    face_y = 0.5 * (padded[1:-1, 1:, 1:-1] + padded[1:-1, :-1, 1:-1])
    face_z = 0.5 * WEIGHT_Z * (padded[1:-1, 1:-1, 1:] + padded[1:-1, 1:-1, :-1])
    diagonal = (
        face_x[:-1]
        + face_x[1:]
        + face_y[:, :-1]
        + face_y[:, 1:]
        + face_z[:, :, :-1]
        + face_z[:, :, 1:]
    )
    return (face_x, face_y, face_z, diagonal)


def neighbors(basis, face_x, face_y, face_z):
    padded = jnp.pad(basis, ((0, 0), (1, 1), (1, 1), (1, 1)))
    total = face_x[1:] * padded[:, 2:, 1:-1, 1:-1] + face_x[:-1] * padded[:, :-2, 1:-1, 1:-1]
    total = (
        total
        + face_y[:, 1:] * padded[:, 1:-1, 2:, 1:-1]
        + face_y[:, :-1] * padded[:, 1:-1, :-2, 1:-1]
    )
    total = (
        total
        + face_z[:, :, 1:] * padded[:, 1:-1, 1:-1, 2:]
        + face_z[:, :, :-1] * padded[:, 1:-1, 1:-1, :-2]
    )
    return total


def couple(basis, face_x, face_y, face_z, diagonal, beyond):
    length_x, length_y, length_z = (basis.shape[1], basis.shape[2], basis.shape[3])
    shape_blocks = (length_x // B, B, length_y // B, B, length_z)

    def tiles(values):
        return values.reshape(values.shape[:-3] + shape_blocks)

    def contract(left, right):
        lines = jnp.einsum("cixjyz,eixjyz->ceijz", left, right, precision=lax.Precision.HIGHEST)
        return jnp.sum(lines.reshape(lines.shape[:-1] + (length_z // B, B)), axis=-1)

    place_z = jnp.arange(length_z, dtype=jnp.int32) % B
    last_z = (place_z == B - 1).astype(basis.dtype)
    inner_mask = 1.0 - last_z
    tiled = tiles(basis)
    self_terms = contract(tiled * tiles(diagonal), tiled)
    upper_x = tiles(jnp.concatenate([basis[:, 1:], beyond[:, None]], axis=1))
    upper_y = tiles(jnp.pad(basis[:, :, 1:], ((0, 0), (0, 0), (0, 1), (0, 0))))
    upper_z = tiles(jnp.pad(basis[:, :, :, 1:], ((0, 0), (0, 0), (0, 0), (0, 1))))
    weight_x = tiles(face_x[1:]) * tiled
    weight_y = tiles(face_y[:, 1:]) * tiled
    weight_z = tiles(face_z[:, :, 1:]) * tiled
    inner_x = contract(weight_x[:, :, : B - 1], upper_x[:, :, : B - 1])
    cross_x = contract(weight_x[:, :, B - 1 :], upper_x[:, :, B - 1 :])
    inner_y = contract(weight_y[:, :, :, :, : B - 1], upper_y[:, :, :, :, : B - 1])
    cross_y = contract(weight_y[:, :, :, :, B - 1 :], upper_y[:, :, :, :, B - 1 :])
    inner_z = contract(weight_z * inner_mask, upper_z)
    cross_z = contract(weight_z * last_z, upper_z)
    inner_sum = inner_x + inner_y + inner_z
    block_part = self_terms - inner_sum - jnp.transpose(inner_sum, (1, 0, 2, 3, 4))
    face_part = -jnp.stack([cross_x, cross_y, cross_z])
    return (block_part / B**3, face_part / B**2)


def on_device(permeability, sources):
    width_x = permeability.shape[0]
    perm_ext = extended_2(permeability, (("gx", 0),), 1)
    full_x, full_y, full_z, full_diag = conduct(perm_ext)
    face_x = full_x[1 : width_x + 2]
    face_y = full_y[1 : width_x + 1]
    face_z = full_z[1 : width_x + 1]
    diagonal = full_diag[1 : width_x + 1]
    basis = sources / diagonal
    for repeat in range(SWEEPS - 1):
        extended = extended_2(basis, (("gx", 1),), 1)
        total = neighbors(extended, full_x, full_y, full_z)[:, 1 : width_x + 1]
        basis = (sources + total) / diagonal
    beyond = from_behind(basis[:, 0], "gx", -1)
    return couple(basis, face_x, face_y, face_z, diagonal, beyond)


def solution(mesh):
    placed = (P("gx", "grp", None), P(None, "gx", "grp", None))
    return jax.shard_map(
        on_device,
        mesh=mesh,
        in_specs=placed,
        out_specs=(P(None, None, "gx", "grp", None), P(None, None, None, "gx", "grp", None)),
        check_vma=False,
    )
```

profile of v0, /device:TPU:9, one launch (start us, length us, event | category | flops | bytes accessed | tf_op | source)
XLA Modules:
  0.0 429.1 jit_solution(11852336120284738953)
XLA Ops:
  1.4 3.7 collective-permute-start
  19.0 4.6 %collective-permute-done.3 = f32[8,1,32,128]{3,2,1,0:T(8,128)S(1)} collective-permute-done((f32[8,1,32,128]{3,2,1,0:T(8,128)S(1)}, f32[8,1,32,128]{3,2,1,0:T(8,128)S(1)}, u32[]{:S(2)}, u32[]{:S(2)}) %collective-permute-start.3) | collective-permute-done | bytes 131104 | tf_op jit(solution)/shard_map/ppermute | solution.py:21
  26.9 6.8 %fusion.58 = (f32[8,18,32,128]{3,2,1,0:T(8,128)}, f32[8,18,32,128]{3,2,1,0:T(8,128)}, f32[8,18,32,128]{3,2,1,0:T(8,128)}, f32[8,18,32,128]{3,2,1,0:T(8,128)}, f3...) fusion(f32[8,20,34,130]{3,2,1,0:T(8,128)S(1)} %select_maximum_fusion.4), kind=kLoop, calls=%fused_computation.115 | loop fusion | bytes 28311552 | tf_op jit(solution)/shard_map/slice | solution.py:50
  33.7 5.7 %fusion.37 = f32[8,16,32,128]{3,2,1,0:T(8,128)S(1)} fusion(f32[8,16,32,128]{3,2,1,0:T(8,128)S(1)} %copy-done, f32[8,18,32,128]{3,2,1,0:T(8,128)} %get-tuple-element.21, f32[8,18,32,128]{3,2,1,0:T(8,128)} %get-tuple-element.17, f32[8,18,32,128]{3,2,1,0:T(8,128)} %get-tuple-element.18, f32[8,18,32,128]{3,2,1,0:T(8,128)} %get-tuple-element.19, ...), kind=kLoop, calls=%fused_computation.66 | loop fusion | flops 6815744 | bytes 18612224 | tf_op jit(solution)/shard_map/div | solution.py:110
  43.8 4.8 %collective-permute-done.5 = f32[8,1,32,128]{3,2,1,0:T(8,128)S(1)} collective-permute-done((f32[8,1,32,128]{3,2,1,0:T(8,128)S(1)}, f32[8,1,32,128]{3,2,1,0:T(8,128)S(1)}, u32[]{:S(2)}, u32[]{:S(2)}) %collective-permute-start.5) | collective-permute-done | bytes 131104 | tf_op jit(solution)/shard_map/ppermute | solution.py:21
  52.0 6.8 %fusion.57 = (f32[8,18,32,128]{3,2,1,0:T(8,128)}, f32[8,18,32,128]{3,2,1,0:T(8,128)}, f32[8,18,32,128]{3,2,1,0:T(8,128)}, f32[8,18,32,128]{3,2,1,0:T(8,128)}, f3...) fusion(f32[8,20,34,130]{3,2,1,0:T(8,128)S(1)} %select_maximum_fusion.2), kind=kLoop, calls=%fused_computation.114 | loop fusion | bytes 28311552 | tf_op jit(solution)/shard_map/slice | solution.py:50
  58.7 6.0 %fusion.30 = f32[8,16,32,128]{3,2,1,0:T(8,128)S(1)} fusion(f32[8,16,32,128]{3,2,1,0:T(8,128)S(1)} %copy-done, f32[8,18,32,128]{3,2,1,0:T(8,128)} %get-tuple-element.15, f32[8,18,32,128]{3,2,1,0:T(8,128)} %get-tuple-element.11, f32[8,18,32,128]{3,2,1,0:T(8,128)} %get-tuple-element.12, f32[8,18,32,128]{3,2,1,0:T(8,128)} %get-tuple-element.13, ...), kind=kLoop, calls=%fused_computation.53 | loop fusion | flops 6815744 | bytes 18612224 | tf_op jit(solution)/shard_map/div | solution.py:110
  82.0 6.8 %fusion.56 = (f32[8,18,32,128]{3,2,1,0:T(8,128)}, f32[8,18,32,128]{3,2,1,0:T(8,128)}, f32[8,18,32,128]{3,2,1,0:T(8,128)}, f32[8,18,32,128]{3,2,1,0:T(8,128)}, f3...) fusion(f32[8,20,34,130]{3,2,1,0:T(8,128)S(1)} %select_maximum_fusion), kind=kLoop, calls=%fused_computation.113 | loop fusion | bytes 28311552 | tf_op jit(solution)/shard_map/slice | solution.py:50
  88.9 6.3 %fusion.23 = f32[8,16,32,128]{3,2,1,0:T(8,128)S(1)} fusion(f32[8,16,32,128]{3,2,1,0:T(8,128)} %param.3, f32[8,18,32,128]{3,2,1,0:T(8,128)} %get-tuple-element.9, f32[8,18,32,128]{3,2,1,0:T(8,128)} %get-tuple-element.5, f32[8,18,32,128]{3,2,1,0:T(8,128)} %get-tuple-element.6, f32[8,18,32,128]{3,2,1,0:T(8,128)} %get-tuple-element.7, ...), kind=kLoop, calls=%fused_computation.40 | loop fusion | flops 6815744 | bytes 18612224 | tf_op jit(solution)/shard_map/div | solution.py:110
  101.0 14.2 %copy.40 = f32[8,1,16,2,16,128]{2,0,4,5,3,1:T(8,128)} copy(f32[8,1,16,2,16,128]{5,4,3,2,0,1:T(8,128)S(1)} %bitcast.95) | data formatting | bytes 4194304 | tf_op jit(solution)/shard_map/reshape | solution.py:69
  115.1 13.6 %copy.36 = f32[8,1,16,2,16,128]{4,0,2,5,3,1:T(8,128)} copy(f32[8,1,16,2,16,128]{5,4,3,2,0,1:T(8,128)S(1)} %bitcast.96) | data formatting | bytes 4194304 | tf_op jit(solution)/shard_map/reshape | solution.py:69
  128.7 4.5 %collective-permute-start.8 = (f32[8,32,128]{2,1,0:T(8,128)}, f32[8,32,128]{2,1,0:T(8,128)S(1)}, u32[]{:S(2)}, u32[]{:S(2)}) collective-permute-start(f32[8,32,128]{2,1,0:T(8,128)} %slice_bitcast_fusion.8), channel_id=1, source_target_pairs={{1,0},{2,1},{3,2},{4,3},{5,4},{6,5},{7,6},{8,7},{9,8},{10,9},{11,1... | collective-permute-start | bytes 393224 | tf_op jit(solution)/shard_map/ppermute | solution.py:29
  138.5 9.2 %copy.37 = f32[8,15,2,16,128]{3,0,1,4,2:T(8,128)} copy(f32[8,15,2,16,128]{4,3,2,1,0:T(8,128)} %bitcast.102) | data formatting | bytes 3932160 | tf_op jit(solution)/shard_map/reshape.5
  147.6 14.5 %copy.45 = f32[8,16,2,16,128]{3,0,1,4,2:T(8,128)} copy(f32[8,16,2,16,128]{4,3,2,1,0:T(8,128)} %bitcast.101) | data formatting | bytes 4194304 | tf_op jit(solution)/shard_map/reshape.27
  162.1 14.7 %copy.61 = f32[8,1,16,2,15,128]{2,0,4,5,3,1:T(8,128)} copy(f32[8,1,16,2,15,128]{5,4,3,2,0,1:T(8,128)} %bitcast.100) | data formatting | bytes 3932160
  176.8 13.6 %copy.34 = f32[8,16,2,16,128]{3,0,1,4,2:T(8,128)} copy(f32[8,16,2,16,128]{4,3,2,1,0:T(8,128)S(1)} %bitcast.97) | data formatting | bytes 4194304 | tf_op jit(solution)/shard_map/reshape.1
  190.4 38.0 %fusion = f32[2,128,8,8,1]{3,2,4,1,0:T(8,128)} fusion(f32[8,16,2,16,128]{3,0,1,4,2:T(8,128)} %copy.34, f32[16,2,16,128]{2,0,3,1:T(8,128)} %copy.32), kind=kOutput, calls=%fused_computation | convolution fusion | flops 50855936 | bytes 2424832 | tf_op jit(solution)/shard_map/cixjyz,eixjyz->ceijz/dot_general | solution.py:72
  229.7 41.7 %fusion.2 = f32[2,128,8,8,1]{3,2,4,1,0:T(8,128)} fusion(f32[8,16,2,16,128]{3,0,1,4,2:T(8,128)} %copy.45, f32[8,16,2,16,128]{3,0,1,4,2:T(8,128)} %copy.34, f32[128]{0:T(128)S(1)} %compare_convert_fusion, f32[16,2,16,128]{2,0,3,1:T(8,128)S(1)} %copy-done.1), kind=kOutput, calls=%fused_computation.2 | convolution fusion | flops 51380224 | bytes 4522496 | tf_op jit(solution)/shard_map/cixjyz,eixjyz->ceijz/dot_general | solution.py:72
  271.4 41.7 %fusion.4 = f32[2,128,8,8,1]{3,2,4,1,0:T(8,128)} fusion(f32[8,16,2,16,128]{3,0,1,4,2:T(8,128)} %copy.45, f32[8,16,2,16,128]{3,0,1,4,2:T(8,128)} %copy.34, f32[128]{0:T(128)S(1)} %broadcast_subtract_fusion, f32[16,2,16,128]{2,0,3,1:T(8,128)S(1)} %copy-done.1), kind=kOutput, calls=%fused_computation.4 | convolution fusion | flops 51380224 | bytes 4522496 | tf_op jit(solution)/shard_map/cixjyz,eixjyz->ceijz/dot_general | solution.py:72
  316.0 12.2 %broadcast_multiply_fusion = f32[8,1,16,2,16,128]{2,0,4,5,3,1:T(8,128)} fusion(f32[8,1,16,2,16,128]{2,0,4,5,3,1:T(8,128)} %copy.40, f32[16,2,16,128]{0,2,3,1:T(8,128)S(1)} %copy-done.4), kind=kLoop, calls=%fused_computation.23 | loop fusion | flops 524288 | bytes 4456448 | tf_op jit(solution)/shard_map/mul | solution.py:84
  328.2 37.4 %fusion.8 = f32[2,128,8,8,1]{3,2,4,1,0:T(8,128)} fusion(f32[8,1,16,2,16,128]{2,0,4,5,3,1:T(8,128)} %broadcast_multiply_fusion, f32[8,1,16,2,15,128]{2,0,4,5,3,1:T(8,128)} %copy.61), kind=kOutput, calls=%fused_computation.9 | convolution fusion | flops 47185920 | bytes 31522816 | tf_op jit(solution)/shard_map/cixjyz,eixjyz->ceijz/dot_general | solution.py:72
  365.6 4.2 fusion.42
  372.4 12.2 %broadcast_multiply_fusion.1 = f32[8,1,16,2,16,128]{4,0,2,5,3,1:T(8,128)} fusion(f32[8,1,16,2,16,128]{4,0,2,5,3,1:T(8,128)} %copy.36, f32[16,2,16,128]{2,0,3,1:T(8,128)S(1)} %copy-done.3), kind=kLoop, calls=%fused_computation.24 | loop fusion | flops 524288 | bytes 4456448 | tf_op jit(solution)/shard_map/mul | solution.py:83
  384.7 38.6 %fusion.9 = f32[2,128,8,8,1]{3,2,4,1,0:T(8,128)S(1)} fusion(f32[8,15,2,16,128]{3,0,1,4,2:T(8,128)} %copy.37, f32[8,1,16,2,16,128]{4,0,2,5,3,1:T(8,128)} %broadcast_multiply_fusion.1), kind=kOutput, calls=%fused_computation.11 | convolution fusion | flops 47185920 | bytes 31522816 | tf_op jit(solution)/shard_map/cixjyz,eixjyz->ceijz/dot_general | solution.py:72
  (97 shorter events, 66.0 us)
Async XLA Ops:
  1.4 5.6 %collective-permute-start = (f32[1,32,128]{2,1,0:T(8,128)S(1)}, f32[1,32,128]{2,1,0:T(8,128)S(1)}, u32[]{:S(2)}, u32[]{:S(2)}) collective-permute-start(f32[1,32,128]{2,1,0:T(8,128)S(1)} %get-tuple-element.40), channel_id=1, source_target_pairs={{0,1},{1,2},{2,3},{3,4},{4,5},{5,6},{6,7},{7,8},{8,9},{9,10},{10,1... | collective-permute-start | bytes 49160 | tf_op jit(solution)/shard_map/ppermute | solution.py:18
  5.1 5.1 %collective-permute-start.1 = (f32[1,32,128]{2,1,0:T(8,128)S(1)}, f32[1,32,128]{2,1,0:T(8,128)S(1)}, u32[]{:S(2)}, u32[]{:S(2)}) collective-permute-start(f32[1,32,128]{2,1,0:T(8,128)S(1)} %get-tuple-element.41), channel_id=1, source_target_pairs={{1,0},{2,1},{3,2},{4,3},{5,4},{6,5},{7,6},{8,7},{9,8},{10,9},{11,1... | collective-permute-start | bytes 49160 | tf_op jit(solution)/shard_map/ppermute | solution.py:21
  12.2 21.5 %copy-start.6 = (f32[16,32,128]{2,1,0:T(8,128)}, f32[16,32,128]{2,1,0:T(8,128)S(1)}, u32[]{:S(2)}) copy-start(f32[16,32,128]{2,1,0:T(8,128)S(1)} %get-tuple-element.28) | copy-start | bytes 786436
  12.2 21.5 %copy-start.8 = (f32[16,32,128]{2,1,0:T(8,128)}, f32[16,32,128]{2,1,0:T(8,128)S(1)}, u32[]{:S(2)}) copy-start(f32[16,32,128]{2,1,0:T(8,128)S(1)} %get-tuple-element.45) | copy-start | bytes 786436
  12.3 21.5 %copy-start.13 = (f32[16,32,128]{2,1,0:T(8,128)}, f32[16,32,128]{2,1,0:T(8,128)S(1)}, u32[]{:S(2)}) copy-start(f32[16,32,128]{2,1,0:T(8,128)S(1)} %get-tuple-element.29) | copy-start | bytes 786436
  12.3 21.5 %copy-start.15 = (f32[16,32,128]{2,1,0:T(8,128)}, f32[16,32,128]{2,1,0:T(8,128)S(1)}, u32[]{:S(2)}) copy-start(f32[16,32,128]{2,1,0:T(8,128)S(1)} %get-tuple-element.44) | copy-start | bytes 786436
  14.5 4.4 %collective-permute-start.2 = (f32[8,1,32,128]{3,2,1,0:T(8,128)S(1)}, f32[8,1,32,128]{3,2,1,0:T(8,128)S(1)}, u32[]{:S(2)}, u32[]{:S(2)}) collective-permute-start(f32[8,1,32,128]{3,2,1,0:T(8,128)S(1)} %get-tuple-element.26), channel_id=1, source_target_pairs={{0,1},{1,2},{2,3},{3,4},{4,5},{5,6},{6,7},{7,8},{8,9},{9,10},{10,1... | collective-permute-start | bytes 393224 | tf_op jit(solution)/shard_map/ppermute | solution.py:18
  16.5 7.1 %collective-permute-start.3 = (f32[8,1,32,128]{3,2,1,0:T(8,128)S(1)}, f32[8,1,32,128]{3,2,1,0:T(8,128)S(1)}, u32[]{:S(2)}, u32[]{:S(2)}) collective-permute-start(f32[8,1,32,128]{3,2,1,0:T(8,128)S(1)} %get-tuple-element.27), channel_id=1, source_target_pairs={{1,0},{2,1},{3,2},{4,3},{5,4},{6,5},{7,6},{8,7},{9,8},{10,9},{11,1... | collective-permute-start | bytes 393224 | tf_op jit(solution)/shard_map/ppermute | solution.py:21
  18.9 14.8 %copy-start.11 = (f32[16,32,128]{2,1,0:T(8,128)}, f32[16,32,128]{2,1,0:T(8,128)S(1)}, u32[]{:S(2)}) copy-start(f32[16,32,128]{2,1,0:T(8,128)S(1)} %get-tuple-element.36) | copy-start | bytes 786436
  39.5 4.3 %collective-permute-start.4 = (f32[8,1,32,128]{3,2,1,0:T(8,128)S(1)}, f32[8,1,32,128]{3,2,1,0:T(8,128)S(1)}, u32[]{:S(2)}, u32[]{:S(2)}) collective-permute-start(f32[8,1,32,128]{3,2,1,0:T(8,128)S(1)} %get-tuple-element.24), channel_id=1, source_target_pairs={{0,1},{1,2},{2,3},{3,4},{4,5},{5,6},{6,7},{7,8},{8,9},{9,10},{10,1... | collective-permute-start | bytes 393224 | tf_op jit(solution)/shard_map/ppermute | solution.py:18
  41.4 7.2 %collective-permute-start.5 = (f32[8,1,32,128]{3,2,1,0:T(8,128)S(1)}, f32[8,1,32,128]{3,2,1,0:T(8,128)S(1)}, u32[]{:S(2)}, u32[]{:S(2)}) collective-permute-start(f32[8,1,32,128]{3,2,1,0:T(8,128)S(1)} %get-tuple-element.25), channel_id=1, source_target_pairs={{1,0},{2,1},{3,2},{4,3},{5,4},{6,5},{7,6},{8,7},{9,8},{10,9},{11,1... | collective-permute-start | bytes 393224 | tf_op jit(solution)/shard_map/ppermute | solution.py:21
  64.8 13.8 %collective-permute-start.6 = (f32[8,1,32,128]{3,2,1,0:T(8,128)S(1)}, f32[8,1,32,128]{3,2,1,0:T(8,128)S(1)}, u32[]{:S(2)}, u32[]{:S(2)}) collective-permute-start(f32[8,1,32,128]{3,2,1,0:T(8,128)S(1)} %get-tuple-element.22), channel_id=1, source_target_pairs={{0,1},{1,2},{2,3},{3,4},{4,5},{5,6},{6,7},{7,8},{8,9},{9,10},{10,1... | collective-permute-start | bytes 393224 | tf_op jit(solution)/shard_map/ppermute | solution.py:18
  66.7 11.9 %collective-permute-start.7 = (f32[8,1,32,128]{3,2,1,0:T(8,128)S(1)}, f32[8,1,32,128]{3,2,1,0:T(8,128)S(1)}, u32[]{:S(2)}, u32[]{:S(2)}) collective-permute-start(f32[8,1,32,128]{3,2,1,0:T(8,128)S(1)} %get-tuple-element.23), channel_id=1, source_target_pairs={{1,0},{2,1},{3,2},{4,3},{5,4},{6,5},{7,6},{8,7},{9,8},{10,9},{11,1... | collective-permute-start | bytes 393224 | tf_op jit(solution)/shard_map/ppermute | solution.py:21
  69.4 5.1 %copy-start.9 = (f32[16,32,128]{2,1,0:T(8,128)S(1)}, f32[16,32,128]{2,1,0:T(8,128)}, u32[]{:S(2)}) copy-start(f32[16,32,128]{2,1,0:T(8,128)} %copy-done.8) | copy-start | bytes 786436
  82.0 6.8 %copy-start.7 = (f32[16,32,128]{2,1,0:T(8,128)S(1)}, f32[16,32,128]{2,1,0:T(8,128)}, u32[]{:S(2)}) copy-start(f32[16,32,128]{2,1,0:T(8,128)} %copy-done.6) | copy-start | bytes 786436
  82.0 6.8 %copy-start.10 = (f32[16,32,128]{2,1,0:T(8,128)S(1)}, f32[16,32,128]{2,1,0:T(8,128)}, u32[]{:S(2)}) copy-start(f32[16,32,128]{2,1,0:T(8,128)} %copy-done.8) | copy-start | bytes 786436
  82.0 6.8 %copy-start.12 = (f32[16,32,128]{2,1,0:T(8,128)S(1)}, f32[16,32,128]{2,1,0:T(8,128)}, u32[]{:S(2)}) copy-start(f32[16,32,128]{2,1,0:T(8,128)} %copy-done.11) | copy-start | bytes 786436
  82.0 6.8 %copy-start.14 = (f32[16,32,128]{2,1,0:T(8,128)S(1)}, f32[16,32,128]{2,1,0:T(8,128)}, u32[]{:S(2)}) copy-start(f32[16,32,128]{2,1,0:T(8,128)} %copy-done.13) | copy-start | bytes 786436
  82.0 6.8 %copy-start.16 = (f32[16,32,128]{2,1,0:T(8,128)S(1)}, f32[16,32,128]{2,1,0:T(8,128)}, u32[]{:S(2)}) copy-start(f32[16,32,128]{2,1,0:T(8,128)} %copy-done.15) | copy-start | bytes 786436
  128.7 7.7 %copy-start.5 = (f32[8,16,31,128]{3,2,1,0:T(8,128)S(1)}, f32[8,16,31,128]{3,2,1,0:T(8,128)}, u32[]{:S(2)}) copy-start(f32[8,16,31,128]{3,2,1,0:T(8,128)} %slice.327) | copy-start | bytes 6094852
  128.7 295.6 %collective-permute-start.8 = (f32[8,32,128]{2,1,0:T(8,128)}, f32[8,32,128]{2,1,0:T(8,128)S(1)}, u32[]{:S(2)}, u32[]{:S(2)}) collective-permute-start(f32[8,32,128]{2,1,0:T(8,128)} %slice_bitcast_fusion.8), channel_id=1, source_target_pairs={{1,0},{2,1},{3,2},{4,3},{5,4},{6,5},{7,6},{8,7},{9,8},{10,9},{11,1... | collective-permute-start | bytes 393224 | tf_op jit(solution)/shard_map/ppermute | solution.py:29
  190.4 39.3 %copy-start.1 = (f32[16,2,16,128]{2,0,3,1:T(8,128)S(1)}, f32[16,2,16,128]{2,0,3,1:T(8,128)}, u32[]{:S(2)}) copy-start(f32[16,2,16,128]{2,0,3,1:T(8,128)} %copy.43) | copy-start | bytes 786436
  313.1 2.8 copy-start.4
  365.6 6.8 %copy-start.3 = (f32[16,2,16,128]{2,0,3,1:T(8,128)S(1)}, f32[16,2,16,128]{2,0,3,1:T(8,128)}, u32[]{:S(2)}) copy-start(f32[16,2,16,128]{2,0,3,1:T(8,128)} %copy.35) | copy-start | bytes 786436
  (2 other events, 3.3 us)
where the time goes:
time: 437 us; the launch traced here: 429 us
  matrix products  205 us (47%)
  local copies, waits for them, and re-layouts  125 us (29%)
  other arithmetic  61.8 us (14%)
  starting transfers between devices  23.3 us (5%)
  waiting for transfers between devices  12.5 us (3%)
    dot_general x7, matrix products, contract(): jnp.einsum('cixjyz,eixjyz->ceijz', left, right, precision=lax.Precision.H...  205 us
    another operation x4, local copies, waits for them, and re-layouts  37.6 us
    reshape x2, local copies, waits for them, and re-layouts, tiles(): return values.reshape(values.shape[:-3] + shape_blocks)  27.7 us
    slice x3, local copies, waits for them, and re-layouts, neighbors(): padded[:, 2:, 1:-1, 1:-1]  20.4 us
    unnamed x38, local copies, waits for them, and re-layouts  19.5 us
    div x3, other arithmetic, on_device(): basis = (sources + total) / diagonal  18 us
    ppermute x4, waiting for transfers between devices, extended_2(): lax.ppermute(lax.slice_in_dim(block, 0, width, axis=dim), axis, backward)  12.5 us
    mul x1, other arithmetic, couple(): weight_x = tiles(face_x[1:]) * tiled  12.2 us
  transfers between devices with their start and end apart: 9, of which 3 were waited for; matrix products, arithmetic and copies ran while one was open for 70% of the time, Pallas kernels for 0%

commit v1 on v0

v1 whole, which is shorter than its diff:
```python
import functools

import jax
import jax.numpy as jnp
from jax import lax
from jax.experimental import pallas as pl
from jax.experimental.pallas import tpu as pltpu
from jax.sharding import PartitionSpec as P

B = 16
WEIGHT_Z = 0.1
NF = 8
NXL = 16
NY = 32
NZ = 128
LO = 3
HI = 4
LAYERS = LO + NXL + HI
ROWS = 8 + NF * NY + 8
NU = 9
F32 = jnp.float32
HIGH = lax.Precision.HIGHEST
MESH = pl.DeviceIdType.MESH


def kernel(n, perm, src, blk_out, face_out,
           K, S, B0, B1, B2, B3, W, U, WX, ACC, CX, CY, VV, VW, RED,
           load_sem, send_sem, recv_sem):
    me = lax.axis_index("gx")
    has_low = me > 0
    has_high = me < n - 1

    barrier = pltpu.get_barrier_semaphore()

    @pl.when(has_low)
    def _():
        pl.semaphore_signal(barrier, inc=1, device_id={"gx": me - 1}, device_id_type=MESH)

    @pl.when(has_high)
    def _():
        pl.semaphore_signal(barrier, inc=1, device_id={"gx": me + 1}, device_id_type=MESH)

    loads = [pltpu.make_async_copy(perm, K.at[pl.ds(LO + 1, NXL), pl.ds(8, NY)], load_sem.at[NF])]
    for c in range(NF):
        loads.append(pltpu.make_async_copy(
            src.at[c], S.at[pl.ds(LO, NXL), pl.ds(c * NY, NY)], load_sem.at[c]))
    for copy in loads:
        copy.start()

    zero8 = jnp.zeros((8, NZ), F32)

    def pads(l, carry):
        K[l, pl.ds(0, 8), :] = zero8
        K[l, pl.ds(8 + NY, 8), :] = zero8
        return carry

    lax.fori_loop(0, LAYERS + 2, pads, 0)

    def pads_b(l, carry):
        base = pl.multiple_of(l * ROWS, 8)
        for ref in (B0, B1, B2, B3):
            ref[pl.ds(base, 8), :] = zero8
            ref[pl.ds(base + ROWS - 8, 8), :] = zero8
        return carry

    lax.fori_loop(0, LAYERS, pads_b, 0)
    for l in (LO - 1, LO + NXL):
        B3[pl.ds(l * ROWS, ROWS), :] = jnp.zeros((ROWS, NZ), F32)
    ACC[...] = jnp.zeros_like(ACC)

    @pl.when(me == 0)
    def _():
        K[pl.ds(0, LO + 1), pl.ds(8, NY), :] = jnp.zeros((LO + 1, NY, NZ), F32)

        def clear(l, carry):
            S[l] = jnp.zeros((NF * NY, NZ), F32)
            return carry

        lax.fori_loop(0, LO, clear, 0)

    @pl.when(me == n - 1)
    def _():
        K[pl.ds(LO + NXL + 1, HI + 1), pl.ds(8, NY), :] = jnp.zeros((HI + 1, NY, NZ), F32)

        def clear(l, carry):
            S[l] = jnp.zeros((NF * NY, NZ), F32)
            return carry

        lax.fori_loop(LO + NXL, LAYERS, clear, 0)

    def up_perm():
        return pltpu.make_async_remote_copy(
            src_ref=K.at[pl.ds(NXL, LO + 1), pl.ds(8, NY)],
            dst_ref=K.at[pl.ds(0, LO + 1), pl.ds(8, NY)],
            send_sem=send_sem.at[0, 0], recv_sem=recv_sem.at[0, 0],
            device_id={"gx": me + 1}, device_id_type=MESH)

    def down_perm():
        return pltpu.make_async_remote_copy(
            src_ref=K.at[pl.ds(LO + 1, HI + 1), pl.ds(8, NY)],
            dst_ref=K.at[pl.ds(LO + NXL + 1, HI + 1), pl.ds(8, NY)],
            send_sem=send_sem.at[1, 0], recv_sem=recv_sem.at[1, 0],
            device_id={"gx": me - 1}, device_id_type=MESH)

    def up_layer(k):
        return pltpu.make_async_remote_copy(
            src_ref=S.at[LO + NXL - k], dst_ref=S.at[LO - k],
            send_sem=send_sem.at[0, k], recv_sem=recv_sem.at[0, k],
            device_id={"gx": me + 1}, device_id_type=MESH)

    def down_layer(k):
        return pltpu.make_async_remote_copy(
            src_ref=S.at[LO - 1 + k], dst_ref=S.at[LO + NXL - 1 + k],
            send_sem=send_sem.at[1, k], recv_sem=recv_sem.at[1, k],
            device_id={"gx": me - 1}, device_id_type=MESH)

    pl.semaphore_wait(barrier, has_low.astype(jnp.int32) + has_high.astype(jnp.int32))

    loads[0].wait()

    @pl.when(has_low)
    def _():
        down_perm().start()

    @pl.when(has_high)
    def _():
        up_perm().start()

    for copy in loads[1:]:
        copy.wait()

    @pl.when(has_low)
    def _():
        for k in range(1, HI + 1):
            down_layer(k).start()

    @pl.when(has_high)
    def _():
        for k in range(1, LO + 1):
            up_layer(k).start()

    lane = lax.broadcasted_iota(jnp.int32, (8, NZ), 1)
    sub = lax.broadcasted_iota(jnp.int32, (8, NZ), 0)
    low_lane = lane == 0
    high_lane = lane == NZ - 1
    place = lane % B
    block_first = place == 0
    block_last = place == B - 1

    def prep(l, own):
        dead = jnp.logical_or(jnp.logical_and(l < LO, me == 0),
                              jnp.logical_and(l >= LO + NXL, me == n - 1))
        alive = jnp.where(dead, 0.0, 1.0).astype(F32)
        x = l - LO
        for t in range(4):
            k = K[l + 1, pl.ds(8 + 8 * t, 8), :]
            fxm = 0.5 * (k + K[l, pl.ds(8 + 8 * t, 8), :])
            fxp = 0.5 * (k + K[l + 2, pl.ds(8 + 8 * t, 8), :])
            fym = 0.5 * (k + K[l + 1, pl.ds(7 + 8 * t, 8), :])
            fyp = 0.5 * (k + K[l + 1, pl.ds(9 + 8 * t, 8), :])
            fzm = (0.5 * WEIGHT_Z) * (k + jnp.where(low_lane, 0.0, pltpu.roll(k, 1, 1)))
            fzp = (0.5 * WEIGHT_Z) * (k + jnp.where(high_lane, 0.0, pltpu.roll(k, NZ - 1, 1)))
            d = fxm + fxp + fym + fyp + fzm + fzp
            inv = jnp.where(alive > 0.5, 1.0 / d, 0.0)
            if t == 0:
                fym = jnp.where(sub == 0, 0.0, fym)
            if t == 3:
                fyp = jnp.where(sub == 7, 0.0, fyp)
            fzm = jnp.where(low_lane, 0.0, fzm)
            fzp = jnp.where(high_lane, 0.0, fzp)
            for q, f in enumerate((fxm, fxp, fym, fyp, fzm, fzp)):
                W[l, q, pl.ds(8 * t, 8), :] = f * inv
            W[l, 6, pl.ds(8 * t, 8), :] = inv
            if own:
                inner_m = jnp.where(x == 0, 0.0, 1.0).astype(F32)
                inner_p = jnp.where(x == NXL - 1, 0.0, 1.0).astype(F32)
                base = pl.multiple_of(x * (NU * NY), 8) + 8 * t

                def put(q, f):
                    U[pl.ds(base + q * NY, 8), :] = f

                put(0, fxm * inner_m)
                put(1, fxp * inner_p)
                put(2, jnp.where(sub == 0, 0.0, fym) if t == 2 else fym)
                put(3, jnp.where(sub == 7, 0.0, fyp) if t == 1 else fyp)
                put(4, jnp.where(block_first, 0.0, fzm))
                put(5, jnp.where(block_last, 0.0, fzp))
                put(6, d)
                spread = jnp.where(block_last, fzp, pltpu.roll(fzp, 1, 1))
                near = jnp.logical_or(block_last, block_first)
                spread = jnp.where(near, spread, pltpu.roll(spread, 2, 1))
                near = jnp.logical_or(block_last, place <= 2)
                spread = jnp.where(near, spread, pltpu.roll(spread, 4, 1))
                near = jnp.logical_or(block_last, place <= 6)
                spread = jnp.where(near, spread, pltpu.roll(spread, 8, 1))
                put(7, spread)
                put(8, fyp)

                @pl.when(x == NXL - 1)
                def _():
                    WX[pl.ds(8 * t, 8), :] = fxp

    def first(l):
        base = pl.multiple_of(l * ROWS, 8) + 8
        for t in range(4):
            inv = W[l, 6, pl.ds(8 * t, 8), :]
            for c in range(NF):
                r = c * NY + 8 * t
                B0[pl.ds(base + r, 8), :] = S[l, pl.ds(r, 8), :] * inv

    def sweep(old, new, l):
        base = pl.multiple_of(l * ROWS, 8) + 8
        for t in range(4):
            wxm, wxp, wym, wyp, wzm, wzp = [W[l, q, pl.ds(8 * t, 8), :] for q in range(6)]
            for c in range(NF):
                r = base + c * NY + 8 * t
                mid = old[pl.ds(r, 8), :]
                x_part = wxm * old[pl.ds(r - ROWS, 8), :] + wxp * old[pl.ds(r + ROWS, 8), :]
                y_part = wym * old[pl.ds(r - 1, 8), :] + wyp * old[pl.ds(r + 1, 8), :]
                z_part = wzm * pltpu.roll(mid, 1, 1) + wzp * pltpu.roll(mid, NZ - 1, 1)
                new[pl.ds(r, 8), :] = (B0[pl.ds(r, 8), :] + x_part) + (y_part + z_part)

    def many(body, start, step, count):
        def run(i, carry):
            body(start + i * step)
            return carry

        lax.fori_loop(0, count, run, 0)

    pairs = [(c, e) for c in range(NF) for e in range(c, NF)]
    near1 = jnp.logical_or(block_last, block_first)
    near2 = jnp.logical_or(block_last, place <= 2)
    near3 = jnp.logical_or(block_last, place <= 6)

    def couple(start, step, count):
        for yb in range(2):
            def run(i, accs):
                l = start + i * step
                x = l - LO
                base = pl.multiple_of(l * ROWS, 8) + 8
                ubase = pl.multiple_of(x * (NU * NY), 8)
                accs = list(accs)
                for tt in range(2):
                    t = 2 * yb + tt
                    u = [U[pl.ds(ubase + q * NY + 8 * t, 8), :] for q in range(7)]
                    bs = [B3[pl.ds(base + c * NY + 8 * t, 8), :] for c in range(NF)]
                    for e in range(NF):
                        r = base + e * NY + 8 * t
                        total = u[6] * bs[e]
                        total -= u[0] * B3[pl.ds(r - ROWS, 8), :] + u[1] * B3[pl.ds(r + ROWS, 8), :]
                        total -= u[2] * B3[pl.ds(r - 1, 8), :] + u[3] * B3[pl.ds(r + 1, 8), :]
                        total -= u[4] * pltpu.roll(bs[e], 1, 1) + u[5] * pltpu.roll(bs[e], NZ - 1, 1)
                        for p, (c, e2) in enumerate(pairs):
                            if e2 == e:
                                accs[p] = accs[p] + bs[c] * total
                    m = [jnp.where(near1, bs[2 * q], pltpu.roll(bs[2 * q + 1], 2, 1)) for q in range(4)]
                    m = [jnp.where(near2, m[2 * q], pltpu.roll(m[2 * q + 1], 4, 1)) for q in range(2)]
                    v = jnp.where(near3, m[0], pltpu.roll(m[1], 8, 1))
                    vr = pl.ds(pl.multiple_of(yb * 256 + x * 16, 8) + 8 * tt, 8)
                    VV[vr, :] = v
                    VW[vr, :] = v * U[pl.ds(ubase + 7 * NY + 8 * t, 8), :]
                return tuple(accs)

            accs = tuple(ACC[yb, p] for p in range(len(pairs)))
            accs = lax.fori_loop(0, count, run, accs)
            for p in range(len(pairs)):
                ACC[yb, p] = accs[p]

    def prep_first(l):
        prep(l, True)
        first(l)

    many(prep_first, LO + 1, 1, NXL - 2)
    many(functools.partial(sweep, B0, B1), LO + 2, 1, NXL - 4)
    many(functools.partial(sweep, B1, B2), LO + 3, 1, NXL - 6)
    many(functools.partial(sweep, B2, B3), LO + 4, 1, NXL - 8)
    couple(LO + 5, 1, NXL - 10)

    @pl.when(has_low)
    def _():
        up_perm().wait_recv()

    @pl.when(has_high)
    def _():
        down_perm().wait_recv()

    many(prep_first, LO, NXL - 1, 2)
    many(lambda l: prep(l, False), 0, 1, LO)
    many(lambda l: prep(l, False), LO + NXL, 1, HI)

    def stage(k, carry):
        @pl.when(jnp.logical_and(has_low, k > 0))
        def _():
            up_layer(k).wait_recv()

        @pl.when(jnp.logical_and(has_high, k > 0))
        def _():
            down_layer(k).wait_recv()

        @pl.when(k > 0)
        def _():
            many(first, LO - k, NXL - 1 + 2 * k, 2)

        many(functools.partial(sweep, B0, B1), LO + 1 - k, NXL - 3 + 2 * k, 2)
        many(functools.partial(sweep, B1, B2), LO + 2 - k, NXL - 5 + 2 * k, 2)
        many(functools.partial(sweep, B2, B3), LO + 3 - k, NXL - 7 + 2 * k, 2)
        couple(LO + 4 - k, NXL - 9 + 2 * k, 2)
        return carry

    lax.fori_loop(0, LO + 1, stage, 0)
    couple(LO, NXL - 1, 2)

    for h in range(2):
        def rows(ref, first_row, stride):
            return ref[pl.ds(first_row, 8, stride=stride), :]

        wy = rows(U, (8 * h * NU + 8) * NY + B - 1, NU * NY)
        left = [wy * rows(B3, (LO + 8 * h) * ROWS + 8 + c * NY + B - 1, ROWS) for c in range(NF)]
        right = [rows(B3, (LO + 8 * h) * ROWS + 8 + e * NY + B, ROWS) for e in range(NF)]
        for c in range(NF):
            for e in range(NF):
                value = left[c] * right[e]
                if h == 0:
                    CY[pl.ds((c * NF + e) * 8, 8), :] = value
                else:
                    CY[pl.ds((c * NF + e) * 8, 8), :] += value

    @pl.when(has_high)
    def _():
        down_layer(HI).wait_recv()

    first(LO + NXL + 3)
    sweep(B0, B1, LO + NXL + 2)
    sweep(B1, B2, LO + NXL + 1)
    sweep(B2, B3, LO + NXL)

    base = (LO + NXL - 1) * ROWS + 8
    for yb in range(2):
        def pick(layer, c, tt):
            return B3[pl.ds(base + layer * ROWS + c * NY + 16 * yb + 8 * tt, 8), :]

        right = [[pick(1, e, tt) for e in range(NF)] for tt in range(2)]
        wx = [WX[pl.ds(16 * yb + 8 * tt, 8), :] for tt in range(2)]
        for c in range(NF):
            left = [wx[tt] * pick(0, c, tt) for tt in range(2)]
            for e in range(NF):
                CX[pl.ds(((c * NF + e) * 2 + yb) * 8, 8), :] = left[0] * right[0][e] + left[1] * right[1][e]

    def fold(ref, first_row):
        total = ref[pl.ds(first_row, 8, stride=8), :]
        for s in range(1, 8):
            total = total + ref[pl.ds(first_row + s, 8, stride=8), :]
        return total

    zi = lax.broadcasted_iota(jnp.int32, (NZ, NZ), 0)
    zj = lax.broadcasted_iota(jnp.int32, (NZ, NZ), 1)
    group = (zi // B == zj).astype(F32)

    for yb in range(2):
        for p, (c, e) in enumerate(pairs):
            value = ACC[yb, p]
            RED[pl.ds(((c * NF + e) * 2 + yb) * 8, 8), :] = value
            if c != e:
                RED[pl.ds(((e * NF + c) * 2 + yb) * 8, 8), :] = value

    def dot(a, b):
        return lax.dot_general(a, b, (((1,), (0,)), ((), ())), precision=HIGH, preferred_element_type=F32)

    blk = jnp.concatenate([fold(RED, 64 * q) for q in range(16)], axis=0)
    blk_out[...] = dot(blk, group)[:, :8] * (1.0 / B**3)
    fx = jnp.concatenate([fold(CX, 64 * q) for q in range(16)], axis=0)
    face_out[pl.ds(0, 128), :] = dot(fx, group)[:, :8] * (-1.0 / B**2)

    fy = jnp.concatenate([fold(CY, 64 * q) for q in range(8)], axis=0)
    fy = dot(fy, group) * (-1.0 / B**2)
    zeros64 = jnp.zeros((64, NZ), F32)
    RED[pl.ds(0, 64, stride=2), :] = fy
    RED[pl.ds(1, 64, stride=2), :] = zeros64

    def slot(z):
        s = lax.rem(z - (B - 1) + NZ, NZ)
        return s // B, (s % B) // 2, s % 2

    ij, ic, ip = slot(zi)
    jj, je, jp = slot(zj)
    keep = jnp.logical_and(jnp.logical_and(ij == jj, ij < NZ // B - 1), jnp.logical_and(ip == 0, jp == 1))
    spread = jnp.logical_and(ip == 1, zj == ic * 8 + ij).astype(F32)
    wide = lax.broadcasted_iota(jnp.int32, (8, NZ), 1)
    wj, wc, wp = slot(wide)
    gather = jnp.logical_and(wp == 0, wc == lax.broadcasted_iota(jnp.int32, (8, NZ), 0)).astype(F32)
    for yb in range(2):
        gram = lax.dot_general(VV[pl.ds(yb * 256, 256), :], VW[pl.ds(yb * 256, 256), :],
                               (((0,), (0,)), ((), ())), precision=HIGH, preferred_element_type=F32)
        gram = jnp.where(keep, gram, 0.0)
        out = dot(gather, dot(gram, spread)) * (-1.0 / B**2)
        for e in range(NF):
            value = out if e == 0 else pltpu.roll(out, NZ - 8 * e, 1)
            RED[pl.ds(128 + e * 2 + yb, 8, stride=16), :] = value
    face_out[pl.ds(128, 256), :] = RED[pl.ds(0, 256), :][:, :8]

    @pl.when(has_low)
    def _():
        down_perm().wait_send()
        for k in range(1, HI + 1):
            down_layer(k).wait_send()

    @pl.when(has_high)
    def _():
        up_perm().wait_send()
        for k in range(1, LO + 1):
            up_layer(k).wait_send()


def on_device(n, permeability, sources):
    blk, face = pl.pallas_call(
        functools.partial(kernel, n),
        out_shape=(jax.ShapeDtypeStruct((NF * NF * 2, 8), F32),
                   jax.ShapeDtypeStruct((3 * NF * NF * 2, 8), F32)),
        in_specs=[pl.BlockSpec(memory_space=pl.ANY)] * 2,
        out_specs=(pl.BlockSpec(memory_space=pltpu.VMEM),) * 2,
        scratch_shapes=[
            pltpu.VMEM((LAYERS + 2, NY + 16, NZ), F32),
            pltpu.VMEM((LAYERS, NF * NY, NZ), F32),
            pltpu.VMEM((LAYERS * ROWS, NZ), F32),
            pltpu.VMEM((LAYERS * ROWS, NZ), F32),
            pltpu.VMEM((LAYERS * ROWS, NZ), F32),
            pltpu.VMEM((LAYERS * ROWS, NZ), F32),
            pltpu.VMEM((LAYERS, 7, NY, NZ), F32),
            pltpu.VMEM((NXL * NU * NY, NZ), F32),
            pltpu.VMEM((NY, NZ), F32),
            pltpu.VMEM((2, 36, 8, NZ), F32),
            pltpu.VMEM((NF * NF * 2 * 8, NZ), F32),
            pltpu.VMEM((NF * NF * 8, NZ), F32),
            pltpu.VMEM((512, NZ), F32),
            pltpu.VMEM((512, NZ), F32),
            pltpu.VMEM((NF * NF * 2 * 8, NZ), F32),
            pltpu.SemaphoreType.DMA((NF + 1,)),
            pltpu.SemaphoreType.DMA((2, HI + 1)),
            pltpu.SemaphoreType.DMA((2, HI + 1)),
        ],
        compiler_params=pltpu.CompilerParams(
            collective_id=0, has_side_effects=True, vmem_limit_bytes=40 * 1024 * 1024),
    )(permeability, sources)
    return blk.reshape(NF, NF, 1, 2, 8), face.reshape(3, NF, NF, 1, 2, 8)


def solution(mesh):
    return jax.shard_map(
        functools.partial(on_device, mesh.shape["gx"]),
        mesh=mesh,
        in_specs=(P("gx", "grp", None), P(None, "gx", "grp", None)),
        out_specs=(P(None, None, "gx", "grp", None), P(None, None, None, "gx", "grp", None)),
        check_vma=False,
    )
```

time: 437 us -> 47 us (0.11)
  the two profiles are of different devices: /device:TPU:9 before, /device:TPU:1 now
where the time goes in v1:
time: 47 us; the launch traced here: 46.8 us
  Pallas kernels  42.3 us (90%)
  local copies, waits for them, and re-layouts  3.84 us (8%)
  between operations  0.65 us (1%)
    pallas_call x1, Pallas kernels, on_device(): pl.pallas_call(functools.partial(kernel, n), out_shape=(jax.ShapeDtypeStr...  42.3 us
    unnamed x6, local copies, waits for them, and re-layouts  3.84 us

profile of v1, /device:TPU:1, one launch (start us, length us, event | category | flops | bytes accessed | tf_op | source)
XLA Modules:
  0.0 46.8 jit_solution(2474021454259555957)
XLA Ops:
  0.6 0.0 copy-start
  0.6 1.6 %copy-done = f32[8,16,32,128]{3,2,1,0:T(8,128)S(1)} copy-done((f32[8,16,32,128]{3,2,1,0:T(8,128)S(1)}, f32[8,16,32,128]{3,2,1,0:T(8,128)}, u32[]{:S(2)}) %copy-start) | copy-done | bytes 2097176
  2.2 0.0 copy-start.1
  2.2 0.9 %copy-done.1 = f32[16,32,128]{2,1,0:T(8,128)S(1)} copy-done((f32[16,32,128]{2,1,0:T(8,128)S(1)}, f32[16,32,128]{2,1,0:T(8,128)}, u32[]{:S(2)}) %copy-start.1) | copy-done | bytes 262168
  3.2 42.3 %shard_map.41 = (f32[128,8]{1,0:T(8,128)S(1)}, f32[384,8]{1,0:T(8,128)S(1)}) custom-call(f32[16,32,128]{2,1,0:T(8,128)S(1)} %copy-done.1, f32[8,16,32,128]{3,2,1,0:T(8,128)S(1)} %copy-done), custom_call_target="tpu_custom_call" | custom-call | tf_op jit(solution)/shard_map/pallas_call | solution.py:415
  45.5 0.6 %copy.8 = f32[8,8,1,2,8]{4,3,2,1,0:T(2,128)} copy(f32[8,8,1,2,8]{4,3,2,1,0:T(2,128)S(1)} %bitcast.7) | data formatting | bytes 8192
  46.2 0.7 %copy.9 = f32[3,8,8,1,2,8]{5,4,3,2,1,0:T(2,128)} copy(f32[3,8,8,1,2,8]{5,4,3,2,1,0:T(2,128)S(1)} %bitcast.6) | data formatting | bytes 24576
Async XLA Ops:
  0.6 1.6 %copy-start = (f32[8,16,32,128]{3,2,1,0:T(8,128)S(1)}, f32[8,16,32,128]{3,2,1,0:T(8,128)}, u32[]{:S(2)}) copy-start(f32[8,16,32,128]{3,2,1,0:T(8,128)} %src.1) | copy-start | bytes 6291460
  2.2 0.9 %copy-start.1 = (f32[16,32,128]{2,1,0:T(8,128)S(1)}, f32[16,32,128]{2,1,0:T(8,128)}, u32[]{:S(2)}) copy-start(f32[16,32,128]{2,1,0:T(8,128)} %perm.1) | copy-start | bytes 786436

commit v2 on v1

--- a/solution.py
+++ b/solution.py
@@ -24,7 +24,7 @@
 
 
 def kernel(n, perm, src, blk_out, face_out,
-           K, S, B0, B1, B2, B3, W, U, WX, ACC, CX, CY, VV, VW, RED,
+           K, S, B0, B1, B2, B3, W, U, WX, ACC, CX, CY, VV, VW, RED, TOT,
            load_sem, send_sem, recv_sem):
     me = lax.axis_index("gx")
     has_low = me > 0
@@ -195,10 +195,7 @@
                 spread = jnp.where(near, spread, pltpu.roll(spread, 8, 1))
                 put(7, spread)
                 put(8, fyp)
-
-                @pl.when(x == NXL - 1)
-                def _():
-                    WX[pl.ds(8 * t, 8), :] = fxp
+                WX[pl.ds(8 * t, 8), :] = fxp
 
     def first(l):
         base = pl.multiple_of(l * ROWS, 8) + 8
@@ -270,7 +267,12 @@
         prep(l, True)
         first(l)
 
-    many(prep_first, LO + 1, 1, NXL - 2)
+    def prep_two(l):
+        prep(l, True)
+        prep(l + 1, True)
+
+    many(prep_two, LO + 1, 2, NXL // 2 - 1)
+    many(first, LO + 1, 1, NXL - 2)
     many(functools.partial(sweep, B0, B1), LO + 2, 1, NXL - 4)
     many(functools.partial(sweep, B1, B2), LO + 3, 1, NXL - 6)
     many(functools.partial(sweep, B2, B3), LO + 4, 1, NXL - 8)
@@ -337,20 +339,28 @@
     base = (LO + NXL - 1) * ROWS + 8
     for yb in range(2):
         def pick(layer, c, tt):
-            return B3[pl.ds(base + layer * ROWS + c * NY + 16 * yb + 8 * tt, 8), :]
-
-        right = [[pick(1, e, tt) for e in range(NF)] for tt in range(2)]
-        wx = [WX[pl.ds(16 * yb + 8 * tt, 8), :] for tt in range(2)]
-        for c in range(NF):
-            left = [wx[tt] * pick(0, c, tt) for tt in range(2)]
+            row = c * NY if isinstance(c, int) else pl.multiple_of(c * NY, 8)
+            return B3[pl.ds(row + base + layer * ROWS + 16 * yb + 8 * tt, 8), :]
+
+        def cross(c, carry):
+            left = [WX[pl.ds(16 * yb + 8 * tt, 8), :] * pick(0, c, tt) for tt in range(2)]
             for e in range(NF):
-                CX[pl.ds(((c * NF + e) * 2 + yb) * 8, 8), :] = left[0] * right[0][e] + left[1] * right[1][e]
-
-    def fold(ref, first_row):
-        total = ref[pl.ds(first_row, 8, stride=8), :]
-        for s in range(1, 8):
-            total = total + ref[pl.ds(first_row + s, 8, stride=8), :]
-        return total
+                row = pl.multiple_of(c * (NF * 16), 8) + (e * 2 + yb) * 8
+                CX[pl.ds(row, 8), :] = left[0] * pick(1, e, 0) + left[1] * pick(1, e, 1)
+            return carry
+
+        lax.fori_loop(0, NF, cross, 0)
+
+    def fold(ref, count):
+        def run(q, carry):
+            row = pl.multiple_of(q * 64, 8)
+            parts = [ref[pl.ds(row + k, 8, stride=8), :] for k in range(8)]
+            parts = [parts[k] + parts[k + 4] for k in range(4)]
+            TOT[pl.ds(pl.multiple_of(q * 8, 8), 8), :] = (parts[0] + parts[1]) + (parts[2] + parts[3])
+            return carry
+
+        lax.fori_loop(0, count, run, 0)
+        return TOT[pl.ds(0, 8 * count), :]
 
     zi = lax.broadcasted_iota(jnp.int32, (NZ, NZ), 0)
     zj = lax.broadcasted_iota(jnp.int32, (NZ, NZ), 1)
@@ -366,12 +376,12 @@
     def dot(a, b):
         return lax.dot_general(a, b, (((1,), (0,)), ((), ())), precision=HIGH, preferred_element_type=F32)
 
-    blk = jnp.concatenate([fold(RED, 64 * q) for q in range(16)], axis=0)
+    blk = fold(RED, 16)
     blk_out[...] = dot(blk, group)[:, :8] * (1.0 / B**3)
-    fx = jnp.concatenate([fold(CX, 64 * q) for q in range(16)], axis=0)
+    fx = fold(CX, 16)
     face_out[pl.ds(0, 128), :] = dot(fx, group)[:, :8] * (-1.0 / B**2)
 
-    fy = jnp.concatenate([fold(CY, 64 * q) for q in range(8)], axis=0)
+    fy = fold(CY, 8)
     fy = dot(fy, group) * (-1.0 / B**2)
     zeros64 = jnp.zeros((64, NZ), F32)
     RED[pl.ds(0, 64, stride=2), :] = fy
@@ -434,6 +444,7 @@
             pltpu.VMEM((512, NZ), F32),
             pltpu.VMEM((512, NZ), F32),
             pltpu.VMEM((NF * NF * 2 * 8, NZ), F32),
+            pltpu.VMEM((NF * NF * 2, NZ), F32),
             pltpu.SemaphoreType.DMA((NF + 1,)),
             pltpu.SemaphoreType.DMA((2, HI + 1)),
             pltpu.SemaphoreType.DMA((2, HI + 1)),

time: 47 us -> 28.9 us (0.61)
  Pallas kernels: 42.3 us -> 24.3 us
    pallas_call x1, Pallas kernels: 42.3 us -> 24.3 us  [on_device(): pl.pallas_call(functools.partial(kernel, n), out_shape=(jax.ShapeDtypeStr...]
where the time goes in v2:
time: 28.9 us; the launch traced here: 28.8 us
  Pallas kernels  24.3 us (84%)
  local copies, waits for them, and re-layouts  3.84 us (13%)
  between operations  0.65 us (2%)
    pallas_call x1, Pallas kernels, on_device(): pl.pallas_call(functools.partial(kernel, n), out_shape=(jax.ShapeDtypeStr...  24.3 us
    unnamed x6, local copies, waits for them, and re-layouts  3.84 us

profile of v2, /device:TPU:1, one launch (start us, length us, event | category | flops | bytes accessed | tf_op | source)
XLA Modules:
  0.0 28.8 jit_solution(13692745727600980257)
XLA Ops:
  0.6 0.0 copy-start
  0.6 1.6 %copy-done = f32[8,16,32,128]{3,2,1,0:T(8,128)S(1)} copy-done((f32[8,16,32,128]{3,2,1,0:T(8,128)S(1)}, f32[8,16,32,128]{3,2,1,0:T(8,128)}, u32[]{:S(2)}) %copy-start) | copy-done | bytes 2097176
  2.2 0.0 copy-start.1
  2.2 0.9 %copy-done.1 = f32[16,32,128]{2,1,0:T(8,128)S(1)} copy-done((f32[16,32,128]{2,1,0:T(8,128)S(1)}, f32[16,32,128]{2,1,0:T(8,128)}, u32[]{:S(2)}) %copy-start.1) | copy-done | bytes 262168
  3.2 24.3 %shard_map.41 = (f32[128,8]{1,0:T(8,128)S(1)}, f32[384,8]{1,0:T(8,128)S(1)}) custom-call(f32[16,32,128]{2,1,0:T(8,128)S(1)} %copy-done.1, f32[8,16,32,128]{3,2,1,0:T(8,128)S(1)} %copy-done), custom_call_target="tpu_custom_call" | custom-call | tf_op jit(solution)/shard_map/pallas_call | solution.py:425
  27.5 0.6 %copy.8 = f32[8,8,1,2,8]{4,3,2,1,0:T(2,128)} copy(f32[8,8,1,2,8]{4,3,2,1,0:T(2,128)S(1)} %bitcast.7) | data formatting | bytes 8192
  28.1 0.7 %copy.9 = f32[3,8,8,1,2,8]{5,4,3,2,1,0:T(2,128)} copy(f32[3,8,8,1,2,8]{5,4,3,2,1,0:T(2,128)S(1)} %bitcast.6) | data formatting | bytes 24576
Async XLA Ops:
  0.6 1.6 %copy-start = (f32[8,16,32,128]{3,2,1,0:T(8,128)S(1)}, f32[8,16,32,128]{3,2,1,0:T(8,128)}, u32[]{:S(2)}) copy-start(f32[8,16,32,128]{3,2,1,0:T(8,128)} %src.1) | copy-start | bytes 6291460
  2.2 0.9 %copy-start.1 = (f32[16,32,128]{2,1,0:T(8,128)S(1)}, f32[16,32,128]{2,1,0:T(8,128)}, u32[]{:S(2)}) copy-start(f32[16,32,128]{2,1,0:T(8,128)} %perm.1) | copy-start | bytes 786436

commit v3 on v2

--- a/solution.py
+++ b/solution.py
@@ -219,10 +219,16 @@
 
     def many(body, start, step, count):
         def run(i, carry):
-            body(start + i * step)
+            body(start + 2 * i * step)
+            body(start + (2 * i + 1) * step)
             return carry
 
-        lax.fori_loop(0, count, run, 0)
+        if count == 2:
+            run(0, 0)
+        else:
+            lax.fori_loop(0, count // 2, run, 0)
+        if count % 2:
+            body(start + (count - 1) * step)
 
     pairs = [(c, e) for c in range(NF) for e in range(c, NF)]
     near1 = jnp.logical_or(block_last, block_first)
@@ -267,11 +273,7 @@
         prep(l, True)
         first(l)
 
-    def prep_two(l):
-        prep(l, True)
-        prep(l + 1, True)
-
-    many(prep_two, LO + 1, 2, NXL // 2 - 1)
+    many(lambda l: prep(l, True), LO + 1, 1, NXL - 2)
     many(first, LO + 1, 1, NXL - 2)
     many(functools.partial(sweep, B0, B1), LO + 2, 1, NXL - 4)
     many(functools.partial(sweep, B1, B2), LO + 3, 1, NXL - 6)

time: 28.9 us -> 26.3 us (0.910)
  Pallas kernels: 24.3 us -> 21.6 us
    pallas_call x1, Pallas kernels: 24.3 us -> 21.6 us  [on_device(): pl.pallas_call(functools.partial(kernel, n), out_shape=(jax.ShapeDtypeStr...]
where the time goes in v3:
time: 26.3 us; the launch traced here: 26.1 us
  Pallas kernels  21.6 us (82%)
  local copies, waits for them, and re-layouts  3.84 us (15%)
  between operations  0.65 us (2%)
    pallas_call x1, Pallas kernels, on_device(): pl.pallas_call(functools.partial(kernel, n), out_shape=(jax.ShapeDtypeStr...  21.6 us
    unnamed x6, local copies, waits for them, and re-layouts  3.84 us

profile of v3, /device:TPU:1, one launch (start us, length us, event | category | flops | bytes accessed | tf_op | source)
XLA Modules:
  0.0 26.1 jit_solution(2001311906460075329)
XLA Ops:
  0.6 0.0 copy-start
  0.6 1.6 %copy-done = f32[8,16,32,128]{3,2,1,0:T(8,128)S(1)} copy-done((f32[8,16,32,128]{3,2,1,0:T(8,128)S(1)}, f32[8,16,32,128]{3,2,1,0:T(8,128)}, u32[]{:S(2)}) %copy-start) | copy-done | bytes 2097176
  2.2 0.0 copy-start.1
  2.2 0.9 %copy-done.1 = f32[16,32,128]{2,1,0:T(8,128)S(1)} copy-done((f32[16,32,128]{2,1,0:T(8,128)S(1)}, f32[16,32,128]{2,1,0:T(8,128)}, u32[]{:S(2)}) %copy-start.1) | copy-done | bytes 262168
  3.2 21.6 %shard_map.41 = (f32[128,8]{1,0:T(8,128)S(1)}, f32[384,8]{1,0:T(8,128)S(1)}) custom-call(f32[16,32,128]{2,1,0:T(8,128)S(1)} %copy-done.1, f32[8,16,32,128]{3,2,1,0:T(8,128)S(1)} %copy-done), custom_call_target="tpu_custom_call" | custom-call | tf_op jit(solution)/shard_map/pallas_call | solution.py:427
  24.8 0.6 %copy.8 = f32[8,8,1,2,8]{4,3,2,1,0:T(2,128)} copy(f32[8,8,1,2,8]{4,3,2,1,0:T(2,128)S(1)} %bitcast.7) | data formatting | bytes 8192
  25.4 0.7 %copy.9 = f32[3,8,8,1,2,8]{5,4,3,2,1,0:T(2,128)} copy(f32[3,8,8,1,2,8]{5,4,3,2,1,0:T(2,128)S(1)} %bitcast.6) | data formatting | bytes 24576
Async XLA Ops:
  0.6 1.6 %copy-start = (f32[8,16,32,128]{3,2,1,0:T(8,128)S(1)}, f32[8,16,32,128]{3,2,1,0:T(8,128)}, u32[]{:S(2)}) copy-start(f32[8,16,32,128]{3,2,1,0:T(8,128)} %src.1) | copy-start | bytes 6291460
  2.2 0.9 %copy-start.1 = (f32[16,32,128]{2,1,0:T(8,128)S(1)}, f32[16,32,128]{2,1,0:T(8,128)}, u32[]{:S(2)}) copy-start(f32[16,32,128]{2,1,0:T(8,128)} %perm.1) | copy-start | bytes 786436
